TPU v7x, 128 devices: a whole 4x4x4 slice. The times are simulated.
128 devices in a mesh: side: 2 (over y_hi), row: 8 (over x, y_lo), col: 8 (over z, core).
Axes of the slice: x: 4, y: 4 (y_hi: 2, y_lo: 2; y = y_hi * 2 + y_lo), z: 4, core: 2. Of those that a mesh axis runs over, the one named last changes fastest.
Arguments:
- query_rows: bfloat16 [512, 16384], P(('side', 'row'), 'col'), may hold values from -60 to 60
- key_cache: bfloat16 [512, 256, 1024], P(('side', 'row'), None, 'col'), may hold values from -15 to 15
- value_cache: bfloat16 [512, 256, 1024], P(('side', 'row'), None, 'col'), may hold values from -6 to 6
- cache_lengths: int32 [512], P(('side', 'row')), may hold values from 2 to 256, as said below
- residual_in: bfloat16 [512, 16384], P(('side', 'row'), 'col'), may hold values from -90 to 90
- norm_gain: float32 [16384], replicated, may hold values from 0.5 to 1.5
- outlier_index: int32 [64], replicated, may hold values from 0 to 16383, as said below
- gate_weight: bfloat16 [16384, 26624], P('row', ('side', 'col')), may hold values from -0.046875 to 0.046875
- up_weight: bfloat16 [16384, 26624], P('row', ('side', 'col')), may hold values from -0.046875 to 0.046875
- down_weight: bfloat16 [26624, 16384], P(('side', 'col'), 'row'), may hold values from -0.0390625 to 0.0390625
Outputs:
- layer_out: bfloat16 [512, 16384], P(('side', 'row'), 'col')
Inputs may be any that keep to these rules, and one draw needn't show every extreme that they name: Row i attends to cache entries 0 to cache_lengths[i] - 1; every row whose index is a multiple of 8 is full. `outlier_index`: 64 distinct channels.
All inputs are finite; a program needn't handle non-finite values.
Results may differ from a plain program's by a relative error of at most 0.012.
Values may be sent and summed in bfloat16 or wider, within the bound.
A program may use at most 128 MiB of HBM per device.

v0:
```python
import jax
import jax.numpy as jnp
from jax import lax
from jax.sharding import PartitionSpec as P

HD = 128


def on_device(
    query_rows,
    key_cache,
    value_cache,
    cache_lengths,
    residual_in,
    norm_gain,
    outlier_index,
    gate_weight,
    up_weight,
    down_weight,
):
    rows_dev, width_dev = query_rows.shape
    cache_len = key_cache.shape[1]
    kv_local = key_cache.shape[2] // HD
    group_size = width_dev // HD // kv_local
    query_part = query_rows.reshape(rows_dev, kv_local, group_size, HD)
    key_part = key_cache.reshape(rows_dev, cache_len, kv_local, HD)
    value_part = value_cache.reshape(rows_dev, cache_len, kv_local, HD)
    scores = jnp.einsum(
        "igqd,itgd->igqt", query_part, key_part, preferred_element_type=jnp.float32
    ) * HD ** (-0.5)
    valid_mask = jnp.arange(cache_len, dtype=jnp.int32)[None, :] < cache_lengths[:, None]
    scores = jnp.where(valid_mask[:, None, None, :], scores, -1e30)
    top_score = jnp.max(scores, axis=-1, keepdims=True)
    expon = jnp.exp(scores - top_score)
    attn_probs = (expon / jnp.sum(expon, axis=-1, keepdims=True)).astype(jnp.bfloat16)
    attention = jnp.einsum(
        "igqt,itgd->igqd", attn_probs, value_part, preferred_element_type=jnp.float32
    ).reshape(rows_dev, width_dev)
    residual = (residual_in.astype(jnp.float32) + attention).astype(jnp.bfloat16)
    full_rows = lax.all_to_all(residual, "col", split_axis=0, concat_axis=1, tiled=True)
    resid_f = full_rows.astype(jnp.float32)
    model_width = resid_f.shape[1]
    root_mean = jnp.sqrt(jnp.mean(resid_f * resid_f, axis=1, keepdims=True) + 1e-05)
    normed = resid_f / root_mean * norm_gain[None, :]
    is_outlier = jnp.any(
        jnp.arange(model_width, dtype=jnp.int32)[:, None] == outlier_index[None, :], axis=1
    )
    inliers = jnp.where(is_outlier[None, :], 0.0, jnp.clip(normed, -3.0, 3.0)).astype(jnp.bfloat16)
    outliers = jnp.take(normed, outlier_index, axis=1)
    slices = lax.all_to_all(inliers, "row", split_axis=1, concat_axis=0, tiled=True)
    all_inliers = lax.all_gather(slices, ("side", "col"), axis=0, tiled=True)
    gathered_out = lax.all_gather(outliers, ("side", "row", "col"), axis=0, tiled=True)
    n_side = lax.axis_size("side")
    n_row = lax.axis_size("row")
    n_col = lax.axis_size("col")
    per_device = outliers.shape[0]
    count_out = outliers.shape[1]
    all_outliers = (
        gathered_out.reshape(n_side, n_row, n_col, per_device, count_out)
        .transpose(0, 2, 1, 3, 4)
        .reshape(-1, count_out)
    )
    slice_width = gate_weight.shape[0]
    hidden_width = gate_weight.shape[1]
    local_index = outlier_index - lax.axis_index("row") * slice_width
    inside = ((local_index >= 0) & (local_index < slice_width)).astype(jnp.float32)
    safe_index = jnp.clip(local_index, 0, slice_width - 1)
    gate_rows = jnp.take(gate_weight, safe_index, axis=0).astype(jnp.float32) * inside[:, None]
    up_rows = jnp.take(up_weight, safe_index, axis=0).astype(jnp.float32) * inside[:, None]
    gate_part = jnp.dot(all_inliers, gate_weight, preferred_element_type=jnp.float32) + jnp.dot(
        all_outliers, gate_rows, precision=lax.Precision.HIGHEST
    )
    up_part = jnp.dot(all_inliers, up_weight, preferred_element_type=jnp.float32) + jnp.dot(
        all_outliers, up_rows, precision=lax.Precision.HIGHEST
    )
    gate_up = lax.psum(jnp.concatenate([gate_part, up_part], axis=1), "row")
    hidden_all = (jax.nn.silu(gate_up[:, :hidden_width]) * gate_up[:, hidden_width:]).astype(
        jnp.bfloat16
    )
    ffn_rows = lax.psum_scatter(
        jnp.dot(hidden_all, down_weight, preferred_element_type=jnp.float32).astype(jnp.bfloat16),
        ("side", "col"),
        scatter_dimension=0,
        tiled=True,
    ).astype(jnp.float32)
    returned = lax.all_to_all(
        lax.all_to_all(
            ffn_rows.astype(jnp.bfloat16), "row", split_axis=0, concat_axis=1, tiled=True
        ),
        "col",
        split_axis=1,
        concat_axis=0,
        tiled=True,
    ).astype(ffn_rows.dtype)
    return (residual.astype(jnp.float32) + returned).astype(jnp.bfloat16)


def solution(mesh):
    in_specs = (
        P(("side", "row"), "col"),
        P(("side", "row"), None, "col"),
        P(("side", "row"), None, "col"),
        P(("side", "row")),
        P(("side", "row"), "col"),
        P(),
        P(),
        P("row", ("side", "col")),
        P("row", ("side", "col")),
        P(("side", "col"), "row"),
    )
    out_specs = P(("side", "row"), "col")
    return jax.shard_map(
        on_device, mesh=mesh, in_specs=in_specs, out_specs=out_specs, check_vma=False
    )
```

profile of v0, /device:TPU:7, one launch (start us, length us, event | category | flops | bytes accessed | tf_op | source)
XLA Modules:
  0.0 640.1 jit_solution(10857694206260284155)
XLA Ops:
  6.5 0.0 copy-start
  6.5 0.0 copy-start.3
  6.5 1.1 copy.20
  7.6 0.7 iota_compare_fusion.1
  8.3 0.0 copy-done
  8.4 0.0 copy-start.4
  8.4 0.0 copy-start.2
  8.4 0.7 fusion.8
  9.0 0.2 fusion.34
  9.3 2.5 fusion.18
  11.8 0.0 copy-done.3
  11.8 0.1 fusion.19
  11.9 0.7 all_to_all.42
  12.6 6.0 all-to-all-start
  18.6 0.0 copy-done.4
  18.6 0.7 fusion.2
  19.4 0.0 copy-done.2
  19.5 4.7 gather_fusion.1
  24.2 4.7 gather_fusion.2
  29.0 0.0 all-to-all-done
  29.0 0.2 fusion.17
  29.2 0.9 fusion.27
  30.1 5.2 all-to-all-start.1
  35.3 0.0 all-gather.3.cloned.1.call-start
  35.4 4.7 copy.17
  40.0 0.0 all-to-all-done.1
  40.0 0.7 all_to_all.46
  40.7 0.0 all-gather.3.cloned.1.call-update
  40.7 0.0 all-reduce.2.cloned.1.call-start
  40.8 7.9 %fusion.1 = f32[4,16384]{0,1:T(8,128)} fusion(f32[4,8,2048]{0,2,1:T(8,128)} %copy.17, f32[16384]{0:T(1024)S(1)} %copy-done.2, f32[4]{0:T(128)S(1)} %add_sqrt_fusion), kind=kLoop, calls=%fused_computation.5 | loop fusion | flops 131072 | bytes 589840 | tf_op jit(solution)/shard_map/mul | solution.py:44
  48.7 4.0 gather_fusion
  52.7 0.1 select_bitcast_fusion
  52.7 0.1 copy.18
  52.8 142.3 %all-gather = f32[128,4,64]{2,1,0:T(4,128)S(1)} all-gather(f32[1,4,64]{2,1,0:T(4,128)S(1)} %copy.18), channel_id=1, replica_groups=mesh['side'=2,'row'=8,'col'=8] {'side','row','col'}, dimensions={0}, use_global_device_ids=true | all-gather | bytes 132096 | tf_op jit(solution)/shard_map/all_gather | solution.py:52
  195.1 0.1 copy.19
  195.2 0.0 all-gather.3.cloned.1.call-done
  195.2 7.5 %fusion.35 = f32[512,1664]{1,0:T(8,128)S(1)} fusion(bf16[512,2048]{1,0:T(8,128)(2,1)} %all-gather.3.cloned.1.call-done, bf16[2048,1664]{1,0:T(8,128)(2,1)} %param.19), kind=kOutput, calls=%fused_computation.62 | convolution fusion | flops 3489660928 | bytes 12320768 | tf_op jit(solution)/shard_map/dot_general | solution.py:70
  202.7 0.0 copy-start.5
  202.7 3.1 convolution_add_fusion.1
  205.9 0.0 copy-done.5
  205.9 6.9 %fusion.36 = f32[512,1664]{1,0:T(8,128)S(1)} fusion(bf16[512,2048]{1,0:T(8,128)(2,1)S(1)} %copy-done.5, bf16[2048,1664]{1,0:T(8,128)(2,1)} %param.20), kind=kOutput, calls=%fused_computation.63 | convolution fusion | flops 3489660928 | bytes 12320768 | tf_op jit(solution)/shard_map/dot_general | solution.py:73
  212.8 3.4 convolution_add_fusion
  216.1 3.4 pad_maximum_fusion
  219.5 0.0 all-reduce.2.cloned.1.call-update
  219.5 0.0 reduce-scatter.2.cloned.1.call-start
  219.6 310.9 %all-reduce.2.cloned.1.call-done = f32[512,3328]{1,0:T(8,128)} async-done(((f32[512,3328]{1,0:T(8,128)}), f32[512,3328]{1,0:T(8,128)}) %all-reduce.2.cloned.1.call-update) | async-done | bytes 6815760 | tf_op jit(solution)/shard_map/psum | solution.py:76
  530.5 0.0 copy-start.1
  530.5 10.5 %convolution_convert_fusion = bf16[512,2048]{1,0:T(8,128)(2,1)} fusion(bf16[1664,2048]{1,0:T(8,128)(2,1)} %param.21, f32[512,3328]{1,0:T(8,128)} %all-reduce.2.cloned.1.call-done), kind=kOutput, calls=%fused_computation.13 | convolution fusion | flops 3495821312 | bytes 15728640 | tf_op jit(solution)/shard_map/dot_general | solution.py:81
  541.0 0.0 reduce-scatter.2.cloned.1.call-update
  541.0 70.6 %reduce-scatter.2.cloned.1.call-done = bf16[32,2048]{1,0:T(8,128)(2,1)} async-done(((bf16[512,2048]{1,0:T(8,128)(2,1)}), bf16[32,2048]{1,0:T(8,128)(2,1)}) %reduce-scatter.2.cloned.1.call-update) | async-done | bytes 131088 | tf_op jit(solution)/shard_map/reduce_scatter | solution.py:80
  611.5 1.0 all_to_all.47
  612.5 7.9 %all_to_all.55 = bf16[8,4,2048]{2,1,0:T(4,128)(2,1)S(1)} all-to-all(bf16[8,4,2048]{2,1,0:T(4,128)(2,1)S(1)} %all_to_all.47), channel_id=1, replica_groups=mesh['side'=2,'row'=8,'col'=8] {'row'}, dimensions={0} | all-to-all | bytes 262144 | tf_op jit(solution)/shard_map/all_to_all | solution.py:87
  620.4 12.3 %all_to_all.56 = bf16[4,8,2048]{2,0,1:T(4,128)(2,1)S(1)} all-to-all(bf16[4,8,2048]{2,0,1:T(4,128)(2,1)S(1)} %bitcast.43), channel_id=1, replica_groups=mesh['side'=2,'row'=8,'col'=8] {'col'}, dimensions={1} | all-to-all | bytes 262144 | tf_op jit(solution)/shard_map/all_to_all | solution.py:86
  632.7 0.1 reshape.119
  632.8 0.7 add_convert_fusion
  633.5 0.0 copy-done.1
  (9 shorter events, 0.1 us)
Async XLA Ops:
  6.5 1.8 copy-start
  6.5 5.3 copy-start.3
  8.4 10.3 %copy-start.4 = (s32[64]{0:T(128)S(1)}, s32[64]{0:T(128)}, u32[]{:S(2)}) copy-start(s32[64]{0:T(128)} %param.18) | copy-start | bytes 772
  8.4 11.0 %copy-start.2 = (f32[16384]{0:T(1024)S(1)}, f32[16384]{0:T(1024)}, u32[]{:S(2)}) copy-start(f32[16384]{0:T(1024)} %param.17) | copy-start | bytes 196612
  12.6 16.3 %all-to-all-start = ((bf16[8,4,2048]{2,1,0:T(4,128)(2,1)}), bf16[8,4,2048]{2,1,0:T(4,128)(2,1)S(1)}, u32[]{:S(2)}, u32[]{:S(2)}) async-start(bf16[8,4,2048]{2,1,0:T(4,128)(2,1)} %all_to_all.42), calls=%async_computation | async-start | bytes 262144 | tf_op jit(solution)/shard_map/all_to_all | solution.py:40
  30.1 9.9 %all-to-all-start.1 = ((bf16[4,8,2048]{2,0,1:T(4,128)(2,1)}), bf16[4,8,2048]{2,0,1:T(4,128)(2,1)S(1)}, u32[]{:S(2)}, u32[]{:S(2)}) async-start(bf16[4,8,2048]{2,0,1:T(4,128)(2,1)} %fusion.27), calls=%async_computation.1 | async-start | bytes 262144 | tf_op jit(solution)/shard_map/all_to_all | solution.py:50
  35.3 159.9 %all-gather.3.cloned.1.call-start = ((), (), s32[]{:S(2)}) async-start(), calls=%async_computation.5 | async-start | bytes 2228224 | tf_op jit(solution)/shard_map/all_gather | solution.py:51
  40.7 489.7 %all-reduce.2.cloned.1.call-start = ((), (), s32[]{:S(2)}) async-start(), calls=%async_computation.6 | async-start | bytes 13631488 | tf_op jit(solution)/shard_map/psum | solution.py:76
  202.7 3.1 copy-start.5
  219.5 392.0 %reduce-scatter.2.cloned.1.call-start = ((), (), s32[]{:S(2)}) async-start(), calls=%async_computation.7 | async-start | bytes 2228224 | tf_op jit(solution)/shard_map/reduce_scatter | solution.py:80
  530.5 103.0 %copy-start.1 = (bf16[32,256,128]{2,1,0:T(8,128)(2,1)S(1)}, bf16[32,256,128]{2,1,0:T(8,128)(2,1)}, u32[]{:S(2)}) copy-start(bf16[32,256,128]{2,1,0:T(8,128)(2,1)} %param.13) | copy-start | bytes 6291460
Sparse Core Ops, SparseCore 0:
  40.9 49.4 all-gather.2
  219.6 310.8 all-reduce.1
  541.1 70.3 reduce-scatter.1
where the time goes:
time: 643 us; the launch traced here: 640 us
  waiting for transfers between devices  382 us (59%)
  blocking collectives  163 us (25%)
  matrix products  34.5 us (5%)
  local copies, waits for them, and re-layouts  21.9 us (3%)
  other arithmetic  15 us (2%)
  between operations  13.3 us (2%)
  starting transfers between devices  11.3 us (2%)
    psum x1, waiting for transfers between devices, on_device(): gate_up = lax.psum(jnp.concatenate([gate_part, up_part], axis=1), 'row')  311 us
    all_gather x1, blocking collectives, on_device(): lax.all_gather(outliers, ('side', 'row', 'col'), axis=0, tiled=True)  142 us
    reduce_scatter x1, waiting for transfers between devices, on_device(): lax.psum_scatter(jnp.dot(hidden_all, down_weight, preferred_element_type=...  70.6 us
  transfers between devices with their start and end apart: 5, of which 2 were waited for; matrix products, arithmetic and copies ran while one was open for 4% of the time, Pallas kernels for 0%

commit v1 on v0

v1 whole, which is shorter than its diff:
```python
import functools

import jax
import jax.numpy as jnp
from jax import lax
from jax.experimental import pallas as pl
from jax.experimental.pallas import tpu as pltpu
from jax.sharding import PartitionSpec as P

HD = 128
MESH = pl.DeviceIdType.MESH
STRIPE = 16
TILE = 256
NX = 4
NZ = 4
ORDER = (0, 1, 3, 2)


def ffn_kernel(
    cfg,
    res_ref,
    sq_ref,
    gain_ref,
    mask_ref,
    gate_hbm,
    up_hbm,
    down_hbm,
    out_ref,
    w_in,
    w_out,
    turned,
    sq_buf,
    xbuf,
    gbuf,
    rx1,
    sx,
    rx2,
    ry1,
    sy,
    ry2,
    hbuf,
    obuf,
    rcore,
    osum,
    rz,
    fpeer,
    rside,
    fin,
    rfin,
    w_sem,
    send_sem,
    recv_sem,
    loc_sem,
):
    rows, width, hid = cfg["rows"], cfg["width"], cfg["hid"]
    split_in, split_hid = cfg["split_in"], cfg["split_hid"]
    both = 2 * hid
    s, r, c = lax.axis_index("side"), lax.axis_index("row"), lax.axis_index("col")
    x, p = r // 2, lax.rem(r, 2)
    z, k = c // 2, lax.rem(c, 2)
    diagonal = r == c

    def x_peer(d):
        return (s, lax.rem(x + d, NX) * 2 + p, c)

    def z_peer(d):
        return (s, r, lax.rem(z + d, NZ) * 2 + k)

    y_peer = (s, x * 2 + 1 - p, c)
    side_peer = (1 - s, r, c)
    core_peer = (s, r, z * 2 + 1 - k)
    turn_peer = (s, c, r)

    ids = {}

    def copy(name, src, dst, device):
        i = ids.setdefault(name, len(ids))
        return pltpu.make_async_remote_copy(
            src_ref=src,
            dst_ref=dst,
            send_sem=send_sem.at[i],
            recv_sem=recv_sem.at[i],
            device_id=device,
            device_id_type=MESH,
        )

    sent = []

    def send(name, src, dst, device):
        cp = copy(name, src, dst, device)
        cp.start()
        sent.append(cp)

    def arrive(name, dst):
        copy(name, dst, dst, core_peer).wait_recv()

    w_copies = [
        pltpu.make_async_copy(gate_hbm, w_in.at[:, pl.ds(0, hid)], w_sem.at[0]),
        pltpu.make_async_copy(up_hbm, w_in.at[:, pl.ds(hid, hid)], w_sem.at[1]),
        pltpu.make_async_copy(down_hbm, w_out, w_sem.at[2]),
    ]
    for cp in w_copies:
        cp.start()

    barrier = pltpu.get_barrier_semaphore()
    greet = [x_peer(d) for d in range(1, NX)] + [z_peer(d) for d in range(1, NZ)]
    greet += [y_peer, side_peer, core_peer]
    for device in greet:
        pl.semaphore_signal(barrier, inc=1, device_id=device, device_id_type=MESH)
    for j in range(8):

        @pl.when(jnp.logical_not(jnp.logical_and(diagonal, j == r)))
        def _():
            pl.semaphore_signal(barrier, inc=1, device_id=(s, c, j), device_id_type=MESH)

    pl.semaphore_wait(barrier, len(greet) + 8 - diagonal.astype(jnp.int32))

    turn = copy("turn", res_ref, turned, turn_peer)
    turn_here = pltpu.make_async_copy(res_ref, turned, loc_sem.at[0])
    sq_here = pltpu.make_async_copy(sq_ref, sq_buf.at[c], loc_sem.at[1])
    sq_out = []
    for j in range(8):
        cp = pltpu.make_async_remote_copy(
            src_ref=sq_ref,
            dst_ref=sq_buf.at[c],
            send_sem=send_sem.at[cfg["sq0"] + j],
            recv_sem=recv_sem.at[cfg["sq0"] + c],
            device_id=(s, j, r),
            device_id_type=MESH,
        )
        sq_out.append(cp)

        @pl.when(jnp.logical_not(jnp.logical_and(diagonal, j == r)))
        def _():
            cp.start()

    @pl.when(diagonal)
    def _():
        turn_here.start()
        sq_here.start()
        turn_here.wait()
        sq_here.wait()

    @pl.when(jnp.logical_not(diagonal))
    def _():
        turn.start()

    for j in range(8):

        @pl.when(jnp.logical_not(jnp.logical_and(diagonal, j == c)))
        def _():
            pltpu.make_async_remote_copy(
                src_ref=sq_ref,
                dst_ref=sq_buf.at[j],
                send_sem=send_sem.at[cfg["sq0"] + j],
                recv_sem=recv_sem.at[cfg["sq0"] + j],
                device_id=core_peer,
                device_id_type=MESH,
            ).wait_recv()

    sq_row = jnp.sum(sq_buf[...], axis=0)[0:1, :]
    eye = lax.broadcasted_iota(jnp.int32, (rows, 128), 0) == lax.broadcasted_iota(
        jnp.int32, (rows, 128), 1
    )
    sq_col = jnp.sum(
        jnp.where(eye, jnp.broadcast_to(sq_row, (rows, 128)), 0.0), axis=1, keepdims=True
    )
    inv = 1.0 / jnp.sqrt(sq_col / cfg["model"] + 1e-5)

    @pl.when(jnp.logical_not(diagonal))
    def _():
        turn.wait_recv()

    normed = turned[...].astype(jnp.float32) * inv * gain_ref[...]
    kept = jnp.where(mask_ref[...] > 0.5, normed, jnp.clip(normed, -3.0, 3.0))
    xbuf[0, k, s] = kept.astype(jnp.bfloat16)

    send("g_side", xbuf.at[0, k, s], xbuf.at[0, k, s], side_peer)
    for d in (1, 3, 2):
        send(f"g_z{d}a", xbuf.at[0, k, s], xbuf.at[NZ - d, k, s], z_peer(d))
    send("g_c0a", xbuf.at[0, k, s], xbuf.at[0, k, s], core_peer)
    arrive("g_side", xbuf.at[0, k, 1 - s])
    for d in (1, 3, 2):
        send(f"g_z{d}b", xbuf.at[0, k, 1 - s], xbuf.at[NZ - d, k, 1 - s], z_peer(d))
    send("g_c0b", xbuf.at[0, k, 1 - s], xbuf.at[0, k, 1 - s], core_peer)

    def forward(e):
        d = NZ - e
        arrive(f"g_z{d}a", xbuf.at[e, k, s])
        send(f"g_c{e}a", xbuf.at[e, k, s], xbuf.at[e, k, s], core_peer)
        arrive(f"g_z{d}b", xbuf.at[e, k, 1 - s])
        send(f"g_c{e}b", xbuf.at[e, k, 1 - s], xbuf.at[e, k, 1 - s], core_peer)

    def ready(e):
        arrive(f"g_c{e}a", xbuf.at[e, 1 - k, s])
        arrive(f"g_c{e}b", xbuf.at[e, 1 - k, 1 - s])

    def into_gate_up(e, lo, hi):
        def tile(t, carry):
            cols = pl.ds(pl.multiple_of(t * TILE, TILE), TILE)
            part = jnp.dot(
                xbuf[e].reshape(4 * rows, width),
                w_in[:, cols],
                preferred_element_type=jnp.float32,
            )
            gbuf[e, :, :, :, cols] = part.astype(jnp.bfloat16).reshape(2, NX, STRIPE, TILE)
            return carry

        lax.fori_loop(lo, hi, tile, 0)

    left, right = pl.ds(0, split_in), pl.ds(split_in, both - split_in)

    def reduce_1(e):
        for d in (2, 1, 3):
            send(
                f"rx1_{e}_{d}",
                gbuf.at[e, :, lax.rem(x + d, NX), :, left],
                rx1.at[e, d - 1],
                x_peer(d),
            )
        send(f"ry1_{e}", gbuf.at[e, 1 - p, :, :, right], ry1.at[e], y_peer)

    def f32(value):
        return value.astype(jnp.float32)

    def reduce_2(e):
        arrive(f"ry1_{e}", ry1.at[e])
        sy[e] = (f32(gbuf[e, p, :, :, right]) + f32(ry1[e])).astype(jnp.bfloat16)
        for d in (2, 1, 3):
            send(f"ry2_{e}_{d}", sy.at[e, lax.rem(x + d, NX)], ry2.at[e, d - 1], x_peer(d))
        for d in (1, 3, 2):
            arrive(f"rx1_{e}_{d}", rx1.at[e, d - 1])

        def total(q):
            part = f32(gbuf[e, q, x, :, left])
            for d in (1, 2, 3):
                part = part + f32(rx1[e, d - 1, q])
            return part.astype(jnp.bfloat16)

        sx[e, 1] = total(1 - p)
        send(f"rx2_{e}", sx.at[e, 1], rx2.at[e], y_peer)
        sx[e, 0] = total(p)

    act_a, act_b = pl.ds(0, split_hid), pl.ds(split_hid, hid - split_hid)

    def reduce_3(e):
        arrive(f"rx2_{e}", rx2.at[e])
        lower = f32(sx[e, 0]) + f32(rx2[e])
        for d in (1, 3, 2):
            arrive(f"ry2_{e}_{d}", ry2.at[e, d - 1])
        upper = f32(sy[e, x])
        for d in (1, 2, 3):
            upper = upper + f32(ry2[e, d - 1])
        full = jnp.concatenate([lower, upper], axis=1)
        gate, up = full[:, :hid], full[:, hid:]
        hbuf[e, p, x] = (gate / (1.0 + jnp.exp(-gate)) * up).astype(jnp.bfloat16)
        for d in (2, 1, 3):
            send(f"hx1_{e}_{d}", hbuf.at[e, p, x, :, act_a], hbuf.at[e, p, x, :, act_a], x_peer(d))
        send(f"hy1_{e}", hbuf.at[e, p, x, :, act_b], hbuf.at[e, p, x, :, act_b], y_peer)

    def gather_2(e):
        arrive(f"hy1_{e}", hbuf.at[e, 1 - p, x, :, act_b])
        for d in (2, 1, 3):
            send(f"hx2_{e}_{d}", hbuf.at[e, :, x, :, act_b], hbuf.at[e, :, x, :, act_b], x_peer(d))
        for d in (1, 3, 2):
            arrive(f"hx1_{e}_{d}", hbuf.at[e, p, lax.rem(x + NX - d, NX), :, act_a])
        send(f"hy2_{e}", hbuf.at[e, p, :, :, act_a], hbuf.at[e, p, :, :, act_a], y_peer)

    def down(e):
        for d in (1, 3, 2):
            arrive(f"hx2_{e}_{d}", hbuf.at[e, :, lax.rem(x + NX - d, NX), :, act_b])
        arrive(f"hy2_{e}", hbuf.at[e, 1 - p, :, :, act_a])

        def tile(t, carry):
            cols = pl.ds(pl.multiple_of(t * TILE, TILE), TILE)
            part = jnp.dot(
                hbuf[e].reshape(4 * rows, hid),
                w_out[:, cols],
                preferred_element_type=jnp.float32,
            )
            obuf[e, :, :, :, cols] = part.astype(jnp.bfloat16).reshape(2, 2, rows, TILE)
            return carry

        lax.fori_loop(0, width // TILE, tile, 0)
        send(f"oc_{e}", obuf.at[e, 1 - k], rcore.at[e], core_peer)

    def out_2(e):
        arrive(f"oc_{e}", rcore.at[e])
        osum[e] = (f32(obuf[e, k]) + f32(rcore[e])).astype(jnp.bfloat16)
        if e:
            send(f"oz_{e}", osum.at[e], rz.at[e - 1], z_peer(e))

    tiles = both // TILE
    half = tiles // 2
    ready(0)
    w_copies[0].wait()
    w_copies[1].wait()
    e0, e1, e2, e3 = ORDER
    into_gate_up(e0, 0, half)
    forward(e1)
    into_gate_up(e0, half, tiles)
    reduce_1(e0)
    ready(e1)
    into_gate_up(e1, 0, half)
    forward(e2)
    into_gate_up(e1, half, tiles)
    reduce_1(e1)
    reduce_2(e0)
    ready(e2)
    into_gate_up(e2, 0, half)
    forward(e3)
    into_gate_up(e2, half, tiles)
    reduce_1(e2)
    reduce_2(e1)
    reduce_3(e0)
    ready(e3)
    into_gate_up(e3, 0, tiles)
    reduce_1(e3)
    reduce_2(e2)
    reduce_3(e1)
    gather_2(e0)
    reduce_2(e3)
    reduce_3(e2)
    gather_2(e1)
    w_copies[2].wait()
    down(e0)
    reduce_3(e3)
    gather_2(e2)
    down(e1)
    out_2(e0)
    gather_2(e3)
    down(e2)
    out_2(e1)
    down(e3)
    out_2(e2)
    out_2(e3)

    def block(q):
        part = f32(osum[0, q])
        for d in (1, 2, 3):
            part = part + f32(rz[d - 1, q])
        return part

    for d in (1, 3, 2):
        arrive(f"oz_{d}", rz.at[d - 1])
    fpeer[...] = block(1 - s).astype(jnp.bfloat16)
    send("os", fpeer, rside, side_peer)
    mine = block(s)
    arrive("os", rside)
    fin[...] = (mine + f32(rside[...])).astype(jnp.bfloat16)

    back = copy("back", fin, rfin, turn_peer)
    back_here = pltpu.make_async_copy(fin, rfin, loc_sem.at[0])

    @pl.when(diagonal)
    def _():
        back_here.start()
        back_here.wait()

    @pl.when(jnp.logical_not(diagonal))
    def _():
        back.start()
        back.wait()

    out_ref[...] = (f32(res_ref[...]) + f32(rfin[...])).astype(jnp.bfloat16)

    for cp in sent:
        cp.wait_send()

    @pl.when(jnp.logical_not(diagonal))
    def _():
        turn.wait_send()

    for j in range(8):

        @pl.when(jnp.logical_not(jnp.logical_and(diagonal, j == r)))
        def _():
            sq_out[j].wait_send()


def feed_forward(residual, squares, gain, mask, gate_weight, up_weight, down_weight, model):
    rows, width = residual.shape
    hid = gate_weight.shape[1]
    both = 2 * hid
    split_in = both // TILE * 6 // 13 * TILE
    split_hid = hid // 128 * 7 // 13 * 128
    n_copies = 136
    cfg = dict(
        rows=rows,
        width=width,
        hid=hid,
        split_in=split_in,
        split_hid=split_hid,
        model=model,
        sq0=n_copies,
    )
    bf16 = jnp.bfloat16
    rest = both - split_in
    vmem = pl.BlockSpec(memory_space=pltpu.VMEM)
    hbm = pl.BlockSpec(memory_space=pl.ANY)
    scratch = [
        pltpu.VMEM((width, both), bf16),
        pltpu.VMEM((hid, width), bf16),
        pltpu.VMEM((rows, width), bf16),
        pltpu.VMEM((8, 8, 128), jnp.float32),
        pltpu.VMEM((NZ, 2, 2, rows, width), bf16),
        pltpu.VMEM((NZ, 2, NX, STRIPE, both), bf16),
        pltpu.VMEM((NZ, NX - 1, 2, STRIPE, split_in), bf16),
        pltpu.VMEM((NZ, 2, STRIPE, split_in), bf16),
        pltpu.VMEM((NZ, STRIPE, split_in), bf16),
        pltpu.VMEM((NZ, NX, STRIPE, rest), bf16),
        pltpu.VMEM((NZ, NX, STRIPE, rest), bf16),
        pltpu.VMEM((NZ, NX - 1, STRIPE, rest), bf16),
        pltpu.VMEM((NZ, 2, NX, STRIPE, hid), bf16),
        pltpu.VMEM((NZ, 2, 2, rows, width), bf16),
        pltpu.VMEM((NZ, 2, rows, width), bf16),
        pltpu.VMEM((NZ, 2, rows, width), bf16),
        pltpu.VMEM((NZ - 1, 2, rows, width), bf16),
        pltpu.VMEM((rows, width), bf16),
        pltpu.VMEM((rows, width), bf16),
        pltpu.VMEM((rows, width), bf16),
        pltpu.VMEM((rows, width), bf16),
        pltpu.SemaphoreType.DMA((3,)),
        pltpu.SemaphoreType.DMA((n_copies + 8,)),
        pltpu.SemaphoreType.DMA((n_copies + 8,)),
        pltpu.SemaphoreType.DMA((2,)),
    ]
    return pl.pallas_call(
        functools.partial(ffn_kernel, cfg),
        out_shape=jax.ShapeDtypeStruct((rows, width), bf16),
        in_specs=[vmem, vmem, vmem, vmem, hbm, hbm, hbm],
        out_specs=vmem,
        scratch_shapes=scratch,
        compiler_params=pltpu.CompilerParams(
            collective_id=0, has_side_effects=True, vmem_limit_bytes=60 * 2**20
        ),
    )(residual, squares, gain, mask, gate_weight, up_weight, down_weight)


def on_device(
    query_rows,
    key_cache,
    value_cache,
    cache_lengths,
    residual_in,
    norm_gain,
    outlier_index,
    gate_weight,
    up_weight,
    down_weight,
):
    rows_dev, width_dev = query_rows.shape
    cache_len = key_cache.shape[1]
    kv_local = key_cache.shape[2] // HD
    group_size = width_dev // HD // kv_local
    query_part = query_rows.reshape(rows_dev, kv_local, group_size, HD)
    key_part = key_cache.reshape(rows_dev, cache_len, kv_local, HD)
    value_part = value_cache.reshape(rows_dev, cache_len, kv_local, HD)
    scores = jnp.einsum(
        "igqd,itgd->igqt", query_part, key_part, preferred_element_type=jnp.float32
    ) * HD ** (-0.5)
    valid_mask = jnp.arange(cache_len, dtype=jnp.int32)[None, :] < cache_lengths[:, None]
    scores = jnp.where(valid_mask[:, None, None, :], scores, -1e30)
    top_score = jnp.max(scores, axis=-1, keepdims=True)
    expon = jnp.exp(scores - top_score)
    attn_probs = (expon / jnp.sum(expon, axis=-1, keepdims=True)).astype(jnp.bfloat16)
    attention = jnp.einsum(
        "igqt,itgd->igqd", attn_probs, value_part, preferred_element_type=jnp.float32
    ).reshape(rows_dev, width_dev)
    residual = (residual_in.astype(jnp.float32) + attention).astype(jnp.bfloat16)
    squares = jnp.sum(jnp.square(residual.astype(jnp.float32)), axis=1)
    squares = jnp.zeros((8, 128), jnp.float32).at[0, :rows_dev].set(squares)
    slice_width = gate_weight.shape[0]
    first = lax.axis_index("row") * slice_width
    gain = lax.dynamic_slice(norm_gain, (first,), (slice_width,))[None, :]
    channel = first + jnp.arange(slice_width, dtype=jnp.int32)
    mask = jnp.any(channel[:, None] == outlier_index[None, :], axis=1)
    mask = mask.astype(jnp.float32)[None, :]
    return feed_forward(
        residual, squares, gain, mask, gate_weight, up_weight, down_weight, norm_gain.shape[0]
    )


def solution(mesh):
    in_specs = (
        P(("side", "row"), "col"),
        P(("side", "row"), None, "col"),
        P(("side", "row"), None, "col"),
        P(("side", "row")),
        P(("side", "row"), "col"),
        P(),
        P(),
        P("row", ("side", "col")),
        P("row", ("side", "col")),
        P(("side", "col"), "row"),
    )
    out_specs = P(("side", "row"), "col")
    return jax.shard_map(
        on_device, mesh=mesh, in_specs=in_specs, out_specs=out_specs, check_vma=False
    )
```

time: 643 us -> 119 us (0.19)
  the two profiles are of different devices: /device:TPU:7 before, /device:TPU:3 now
where the time goes in v1:
time: 119 us
  Pallas kernels  108 us (91%)
  local copies, waits for them, and re-layouts  4.55 us (4%)
  matrix products  3.2 us (3%)
  other arithmetic  2.6 us (2%)
    pallas_call x1, Pallas kernels, feed_forward(): pl.pallas_call(functools.partial(ffn_kernel, cfg), out_shape=jax.ShapeDty...  108 us
    unnamed x8, local copies, waits for them, and re-layouts  2.65 us
    dot_general x1, matrix products, on_device(): jnp.einsum('igqt,itgd->igqd', attn_probs, value_part, preferred_element_t...  2.55 us

profile of v1, /device:TPU:3, one launch (start us, length us, event | category | flops | bytes accessed | tf_op | source)
XLA Modules:
  0.0 118.8 jit_solution(1989055753410357957)
XLA Ops:
  0.0 0.0 copy-start
  0.0 1.1 copy.11
  1.1 0.7 iota_compare_fusion
  1.8 0.0 copy-done
  1.8 0.7 fusion.3
  2.5 0.0 copy-start.1
  2.5 0.2 fusion.9
  2.7 0.0 copy-start.2
  2.7 2.6 %fusion.4 = f32[32,16,128]{2,1,0:T(8,128)S(1)} fusion(bf16[32,256,128]{2,1,0:T(8,128)(2,1)} %param.14, f32[32,16]{1,0:T(8,128)S(1)} %fusion.9, f32[32,16,256]{2,1,0:T(8,128)S(1)} %fusion.3), kind=kOutput, calls=%fused_computation.7 | convolution fusion | flops 33948416 | bytes 2885632 | tf_op jit(solution)/shard_map/igqt,itgd->igqd/dot_general | solution.py:467
  5.3 0.0 copy-done.1
  5.3 0.9 multiply_reduce_fusion
  6.1 0.6 scatter.4.sq_ref
  6.7 1.3 %dynamic_slice.3 = f32[2048]{0:T(1024)} dynamic-slice(f32[16384]{0:T(1024)} %param.17, s32[]{:T(128)S(6)} %select_n.9), dynamic_slice_sizes={2048} | dynamic-slice | bytes 16388 | tf_op jit(solution)/shard_map/dynamic_slice | solution.py:475
  8.0 0.0 copy-done.2
  8.0 0.2 compare_reduce_fusion
  8.2 0.6 convert_element_type.32
  8.8 108.4 %shard_map.100 = bf16[32,2048]{1,0:T(8,128)(2,1)} custom-call(bf16[32,2048]{1,0:T(8,128)(2,1)} %get-tuple-element.18.res_ref, f32[8,128]{1,0:T(8,128)} %scatter.4.sq_ref, f32[1,2048]{1,0:T(1,128)} %bitcast.19, f32[1,2048]{1,0:T(1,128)} %bitcast.20, bf16[2048,1664]{1,0:T(8,128)(2,1)} %gate_hbm.1, bf16[2048,1664]{1,0:T(8,128)(2,1)} %up_hbm.1, ...), custom_call_target="tpu_custom_call" | custom-call | tf_op jit(solution)/shard_map/pallas_call | solution.py:428
  117.2 1.6 %copy.16 = bf16[32,2048]{1,0:T(8,128)(2,1)} copy(bf16[32,2048]{1,0:T(8,128)(2,1)} %shard_map.100) | data formatting | bytes 262144
  (1 shorter events, 0.0 us)
Async XLA Ops:
  0.0 1.8 %copy-start = (bf16[32,256,128]{2,1,0:T(8,128)(2,1)S(1)}, bf16[32,256,128]{2,1,0:T(8,128)(2,1)}, u32[]{:S(2)}) copy-start(bf16[32,256,128]{2,1,0:T(8,128)(2,1)} %param.13) | copy-start | bytes 6291460
  2.5 2.8 %copy-start.1 = (bf16[32,2048]{1,0:T(8,128)(2,1)S(1)}, bf16[32,2048]{1,0:T(8,128)(2,1)}, u32[]{:S(2)}) copy-start(bf16[32,2048]{1,0:T(8,128)(2,1)} %param.16) | copy-start | bytes 393220
  2.7 5.3 %copy-start.2 = (s32[64]{0:T(128)S(1)}, s32[64]{0:T(128)}, u32[]{:S(2)}) copy-start(s32[64]{0:T(128)} %param.18) | copy-start | bytes 772

commit v2 on v1

v2 whole, which is shorter than its diff:
```python
import functools

import jax
import jax.numpy as jnp
from jax import lax
from jax.experimental import pallas as pl
from jax.experimental.pallas import tpu as pltpu
from jax.sharding import PartitionSpec as P

HD = 128
MESH = pl.DeviceIdType.MESH
STRIPE = 16
TILE = 256
NX = 4
NZ = 4
ORDER = (0, 1, 3, 2)
RING = (0, 1, 3, 2)
PIECES = 2


def ffn_kernel(
    cfg,
    index_ref,
    res_ref,
    gain_hbm,
    gate_hbm,
    up_hbm,
    down_hbm,
    out_ref,
    w_in,
    w_out,
    gain_ref,
    mask_ref,
    sq_ref,
    turned,
    sq_buf,
    xbuf,
    gbuf,
    rx1,
    sx,
    rx2,
    ry1,
    sy,
    ry2,
    fx,
    fy,
    hbuf,
    obuf,
    rcore,
    osum,
    rz,
    fpeer,
    rside,
    fin,
    w_sem,
    send_sem,
    recv_sem,
    loc_sem,
):
    rows, width, hid = cfg["rows"], cfg["width"], cfg["hid"]
    split_in, split_hid = cfg["split_in"], cfg["split_hid"]
    both = 2 * hid
    s, r, c = lax.axis_index("side"), lax.axis_index("row"), lax.axis_index("col")
    x, p = r // 2, lax.rem(r, 2)
    z, k = c // 2, lax.rem(c, 2)
    diagonal = r == c

    def x_peer(d):
        return (s, lax.rem(x + d, NX) * 2 + p, c)

    def z_peer(d):
        return (s, r, lax.rem(z + d, NZ) * 2 + k)

    y_peer = (s, x * 2 + 1 - p, c)
    side_peer = (1 - s, r, c)
    core_peer = (s, r, z * 2 + 1 - k)
    turn_peer = (s, c, r)

    ids = {}

    def copy(name, src, dst, device):
        i = ids.setdefault(name, len(ids))
        return pltpu.make_async_remote_copy(
            src_ref=src,
            dst_ref=dst,
            send_sem=send_sem.at[i],
            recv_sem=recv_sem.at[i],
            device_id=device,
            device_id_type=MESH,
        )

    sent = []

    def send(name, src, dst, device):
        cp = copy(name, src, dst, device)
        cp.start()
        sent.append(cp)

    def arrive(name, dst):
        copy(name, dst, dst, core_peer).wait_recv()

    w_copies = [
        pltpu.make_async_copy(gate_hbm, w_in.at[:, pl.ds(0, hid)], w_sem.at[0]),
        pltpu.make_async_copy(up_hbm, w_in.at[:, pl.ds(hid, hid)], w_sem.at[1]),
        pltpu.make_async_copy(down_hbm, w_out, w_sem.at[2]),
    ]
    gain_copy = pltpu.make_async_copy(
        gain_hbm.at[:, pl.ds(pl.multiple_of(r * width, width), width)], gain_ref, w_sem.at[3]
    )
    gain_copy.start()
    for cp in w_copies:
        cp.start()

    barrier = pltpu.get_barrier_semaphore()
    greet = [x_peer(d) for d in range(1, NX)] + [z_peer(d) for d in range(1, NZ)]
    greet += [y_peer, side_peer, core_peer]
    for device in greet:
        pl.semaphore_signal(barrier, inc=1, device_id=device, device_id_type=MESH)
    for j in range(8):

        @pl.when(jnp.logical_not(jnp.logical_and(diagonal, j == r)))
        def _():
            pl.semaphore_signal(barrier, inc=1, device_id=(s, c, j), device_id_type=MESH)

    eye = lax.broadcasted_iota(jnp.int32, (rows, 128), 0) == lax.broadcasted_iota(
        jnp.int32, (rows, 128), 1
    )
    sq_part = jnp.sum(jnp.square(res_ref[...].astype(jnp.float32)), axis=1, keepdims=True)
    sq_ref[...] = jnp.broadcast_to(
        jnp.sum(jnp.where(eye, sq_part, 0.0), axis=0, keepdims=True), (8, 128)
    )
    pl.semaphore_wait(barrier, len(greet) + 8 - diagonal.astype(jnp.int32))

    def half(h):
        return pl.ds(h * STRIPE, STRIPE)

    turns = [
        copy(f"turn_{h}", res_ref.at[half(h)], turned.at[half(h)], turn_peer) for h in (0, 1)
    ]
    turn_here = pltpu.make_async_copy(res_ref, turned, loc_sem.at[0])
    sq_here = pltpu.make_async_copy(sq_ref, sq_buf.at[c], loc_sem.at[1])

    @pl.when(jnp.logical_not(diagonal))
    def _():
        turns[0].start()

    sq_out = []
    for j in range(8):
        cp = pltpu.make_async_remote_copy(
            src_ref=sq_ref,
            dst_ref=sq_buf.at[c],
            send_sem=send_sem.at[cfg["sq0"] + j],
            recv_sem=recv_sem.at[cfg["sq0"] + c],
            device_id=(s, j, r),
            device_id_type=MESH,
        )
        sq_out.append(cp)

        @pl.when(jnp.logical_not(jnp.logical_and(diagonal, j == r)))
        def _():
            cp.start()

    @pl.when(diagonal)
    def _():
        turn_here.start()
        sq_here.start()
        turn_here.wait()
        sq_here.wait()

    channel = lax.broadcasted_iota(jnp.int32, (1, width), 1) + r * width

    def match(j, found):
        return jnp.where(channel == index_ref[j], 1.0, found)

    mask_ref[...] = lax.fori_loop(
        0, index_ref.shape[0], match, jnp.zeros((1, width), jnp.float32), unroll=8
    )
    gain_copy.wait()

    @pl.when(jnp.logical_not(diagonal))
    def _():
        turns[0].wait_send()
        turns[1].start()

    for j in range(8):

        @pl.when(jnp.logical_not(jnp.logical_and(diagonal, j == c)))
        def _():
            pltpu.make_async_remote_copy(
                src_ref=sq_ref,
                dst_ref=sq_buf.at[j],
                send_sem=send_sem.at[cfg["sq0"] + j],
                recv_sem=recv_sem.at[cfg["sq0"] + j],
                device_id=core_peer,
                device_id_type=MESH,
            ).wait_recv()

    sq_row = jnp.sum(sq_buf[...], axis=0)[0:1, :]
    sq_col = jnp.sum(
        jnp.where(eye, jnp.broadcast_to(sq_row, (rows, 128)), 0.0), axis=1, keepdims=True
    )
    inv = 1.0 / jnp.sqrt(sq_col / cfg["model"] + 1e-5)

    def first(h):
        @pl.when(jnp.logical_not(diagonal))
        def _():
            turns[h].wait_recv()

        normed = turned[half(h)].astype(jnp.float32) * inv[h * STRIPE : (h + 1) * STRIPE]
        normed = normed * gain_ref[...]
        kept = jnp.where(mask_ref[...] > 0.5, normed, jnp.clip(normed, -3.0, 3.0))
        xbuf[2 * h, k, z] = kept.astype(jnp.bfloat16)
        send(f"g_s{h}", xbuf.at[2 * h, k, z], xbuf.at[2 * h + 1, k, z], side_peer)

    def along_z(e):
        for d in (2, 1, 3):
            send(f"g_z{e}_{d}", xbuf.at[e, k, z], xbuf.at[e, k, z], z_peer(d))

    def second(h):
        arrive(f"g_s{h}", xbuf.at[2 * h + 1, k, z])
        along_z(2 * h + 1)

    def forward(e):
        for d in (1, 3, 2):
            arrive(f"g_z{e}_{d}", xbuf.at[e, k, lax.rem(z + NZ - d, NZ)])
        send(f"g_c{e}", xbuf.at[e, k], xbuf.at[e, k], core_peer)

    def ready(e):
        arrive(f"g_c{e}", xbuf.at[e, 1 - k])

    def into_gate_up(e, lo, hi):
        for t in range(lo, hi):
            cols = pl.ds(t * TILE, TILE)
            part = jnp.dot(
                xbuf[e].reshape(4 * rows, width),
                w_in[:, cols],
                preferred_element_type=jnp.float32,
            )
            gbuf[e, :, :, :, cols] = part.astype(jnp.bfloat16).reshape(2, NX, STRIPE, TILE)

    left, right = pl.ds(0, split_in), pl.ds(split_in, both - split_in)

    def f32(value):
        return value.astype(jnp.float32)

    def halves(lo, size):
        mid = size // 256 * 128
        return pl.ds(lo, mid), pl.ds(lo + mid, size - mid)

    up, far, back_x = (lax.rem(x + d, NX) for d in (1, 2, 3))

    def ring_1(tag, src, land, a, b):
        send(tag + "fa", src(far, a), land(2, a), x_peer(1))
        send(tag + "fb", src(far, b), land(2, b), x_peer(3))
        send(tag + "ub", src(up, b), land(0, b), x_peer(1))
        send(tag + "da", src(back_x, a), land(1, a), x_peer(3))

    def ring_2(tag, src, land, stage, a, b):
        arrive(tag + "fa", land(2, a))
        stage(a)[...] = (f32(land(2, a)[...]) + f32(src(up, a)[...])).astype(jnp.bfloat16)
        send(tag + "ua", stage(a), land(0, a), x_peer(1))
        arrive(tag + "fb", land(2, b))
        stage(b)[...] = (f32(land(2, b)[...]) + f32(src(back_x, b)[...])).astype(jnp.bfloat16)
        send(tag + "db", stage(b), land(1, b), x_peer(3))

    def ring_3(tag, land, a, b):
        arrive(tag + "ub", land(0, b))
        arrive(tag + "da", land(1, a))
        arrive(tag + "ua", land(0, a))
        arrive(tag + "db", land(1, b))

    left_a, left_b = halves(0, split_in)
    rest_a, rest_b = halves(0, both - split_in)

    def x_first(e):
        return (
            f"rx1_{e}",
            lambda i, cols: gbuf.at[e, :, i, :, cols],
            lambda slot, cols: rx1.at[e, slot, :, :, cols],
            lambda cols: fx.at[e, :, :, cols],
        )

    def x_second(e):
        return (
            f"ry2_{e}",
            lambda i, cols: sy.at[e, i, :, cols],
            lambda slot, cols: ry2.at[e, slot, :, cols],
            lambda cols: fy.at[e, :, cols],
        )

    def reduce_1x(e):
        if e in RING:
            tag, src, land, _ = x_first(e)
            ring_1(tag, src, land, left_a, left_b)
            return
        for d in (2, 1, 3):
            send(
                f"rx1_{e}_{d}",
                gbuf.at[e, :, lax.rem(x + d, NX), :, left],
                rx1.at[e, d - 1],
                x_peer(d),
            )

    def reduce_1y(e):
        send(f"ry1_{e}", gbuf.at[e, 1 - p, :, :, right], ry1.at[e], y_peer)

    def x_total(e):
        slots = (0, 1) if e in RING else (0, 1, 2)

        def total(q):
            part = f32(gbuf[e, q, x, :, left])
            for slot in slots:
                part = part + f32(rx1[e, slot, q])
            return part.astype(jnp.bfloat16)

        sx[e, 1] = total(1 - p)
        send(f"rx2_{e}", sx.at[e, 1], rx2.at[e], y_peer)
        sx[e, 0] = total(p)

    def reduce_2(e):
        if e in RING:
            tag, src, land, stage = x_first(e)
            ring_2(tag, src, land, stage, left_a, left_b)
        arrive(f"ry1_{e}", ry1.at[e])
        sy[e] = (f32(gbuf[e, p, :, :, right]) + f32(ry1[e])).astype(jnp.bfloat16)
        if e in RING:
            tag, src, land, _ = x_second(e)
            ring_1(tag, src, land, rest_a, rest_b)
            return
        for d in (2, 1, 3):
            send(f"ry2_{e}_{d}", sy.at[e, lax.rem(x + d, NX)], ry2.at[e, d - 1], x_peer(d))
        for d in (1, 3, 2):
            arrive(f"rx1_{e}_{d}", rx1.at[e, d - 1])
        x_total(e)

    def reduce_2b(e):
        if e not in RING:
            return
        tag, _, land, _ = x_first(e)
        ring_3(tag, land, left_a, left_b)
        x_total(e)
        tag, src, land, stage = x_second(e)
        ring_2(tag, src, land, stage, rest_a, rest_b)

    act_a, act_b = pl.ds(0, split_hid), pl.ds(split_hid, hid - split_hid)
    act_aa, act_ab = halves(0, split_hid)
    act_ba, act_bb = halves(split_hid, hid - split_hid)

    def reduce_3(e):
        arrive(f"rx2_{e}", rx2.at[e])
        lower = f32(sx[e, 0]) + f32(rx2[e])
        upper = f32(sy[e, x])
        if e in RING:
            tag, _, land, _ = x_second(e)
            ring_3(tag, land, rest_a, rest_b)
        for d in (1, 2) if e in RING else (1, 2, 3):
            if e not in RING:
                arrive(f"ry2_{e}_{d}", ry2.at[e, d - 1])
            upper = upper + f32(ry2[e, d - 1])
        full = jnp.concatenate([lower, upper], axis=1)
        gate, up_sum = full[:, :hid], full[:, hid:]
        hbuf[e, p, x] = (gate / (1.0 + jnp.exp(-gate)) * up_sum).astype(jnp.bfloat16)
        for d in (1, 3) if e in RING else (2, 1, 3):
            send(f"hx1_{e}_{d}", hbuf.at[e, p, x, :, act_a], hbuf.at[e, p, x, :, act_a], x_peer(d))
        send(f"hy1_{e}", hbuf.at[e, p, x, :, act_b], hbuf.at[e, p, x, :, act_b], y_peer)

    def row_a(e, i, cols):
        return hbuf.at[e, p, i, :, cols]

    def row_b(e, i, cols):
        return hbuf.at[e, :, i, :, cols]

    def pass_on(e, tag, row, whole, a, b):
        arrive(f"{tag}_{e}_1", row(e, back_x, whole))
        send(f"{tag}_{e}_a", row(e, back_x, a), row(e, back_x, a), x_peer(1))
        arrive(f"{tag}_{e}_3", row(e, up, whole))
        send(f"{tag}_{e}_b", row(e, up, b), row(e, up, b), x_peer(3))

    def passed_on(e, tag, row, a, b):
        arrive(f"{tag}_{e}_a", row(e, far, a))
        arrive(f"{tag}_{e}_b", row(e, far, b))

    def gather_2(e):
        if e in RING:
            pass_on(e, "hx1", row_a, act_a, act_aa, act_ab)
        arrive(f"hy1_{e}", hbuf.at[e, 1 - p, x, :, act_b])
        for d in (1, 3) if e in RING else (2, 1, 3):
            send(f"hx2_{e}_{d}", row_b(e, x, act_b), row_b(e, x, act_b), x_peer(d))
        if e in RING:
            return
        for d in (1, 3, 2):
            arrive(f"hx1_{e}_{d}", row_a(e, lax.rem(x + NX - d, NX), act_a))
        send(f"hy2_{e}", hbuf.at[e, p, :, :, act_a], hbuf.at[e, p, :, :, act_a], y_peer)

    def gather_2b(e):
        if e not in RING:
            return
        passed_on(e, "hx1", row_a, act_aa, act_ab)
        send(f"hy2_{e}", hbuf.at[e, p, :, :, act_a], hbuf.at[e, p, :, :, act_a], y_peer)
        pass_on(e, "hx2", row_b, act_b, act_ba, act_bb)

    def down_ready(e):
        if e in RING:
            passed_on(e, "hx2", row_b, act_ba, act_bb)
        else:
            for d in (1, 3, 2):
                arrive(f"hx2_{e}_{d}", row_b(e, lax.rem(x + NX - d, NX), act_b))
        arrive(f"hy2_{e}", hbuf.at[e, 1 - p, :, :, act_a])

    def down_tiles(e, lo, hi):
        for t in range(lo, hi):
            cols = pl.ds(t * TILE, TILE)
            part = jnp.dot(
                hbuf[e].reshape(4 * rows, hid),
                w_out[:, cols],
                preferred_element_type=jnp.float32,
            )
            obuf[e, :, :, :, cols] = part.astype(jnp.bfloat16).reshape(2, NZ, STRIPE, TILE)

    def down(e):
        down_ready(e)
        down_tiles(e, 0, width // TILE)
        send(f"oc_{e}", obuf.at[e, 1 - k], rcore.at[e], core_peer)

    def out_2(e, name, cols):
        arrive(f"oc_{name}", rcore.at[e, :, :, cols])
        osum[e, :, :, cols] = (f32(obuf[e, k, :, :, cols]) + f32(rcore[e, :, :, cols])).astype(
            jnp.bfloat16
        )
        for d in (2, 1, 3):
            send(
                f"oz_{name}_{d}",
                osum.at[e, lax.rem(z + d, NZ), :, cols],
                rz.at[e, d - 1, :, cols],
                z_peer(d),
            )

    def z_sum(e, name, cols):
        part = f32(osum[e, z, :, cols])
        for d in (1, 3, 2):
            arrive(f"oz_{name}_{d}", rz.at[e, d - 1, :, cols])
            part = part + f32(rz[e, d - 1, :, cols])
        return part

    backs = []

    def out_3(e, name, cols):
        h, part = e // 2, z_sum(e, name, cols)
        if e % 2:
            fpeer[half(h), cols] = part.astype(jnp.bfloat16)
            send(f"os_{h}", fpeer.at[half(h), cols], rside.at[half(h), cols], side_peer)
            return
        if all(back_h != h for back_h, _ in backs):
            arrive(f"os_{h}", rside.at[half(h)])
        fin[half(h), cols] = (part + f32(rside[half(h), cols])).astype(jnp.bfloat16)
        back = copy(
            f"back_{name}", fin.at[half(h), cols], out_ref.at[half(h), cols], turn_peer
        )
        backs.append((h, back))

        @pl.when(jnp.logical_not(diagonal))
        def _():
            back.start()

    tiles = both // TILE
    cut = split_in // TILE

    def gate_up(e, then=None):
        ready(e)
        into_gate_up(e, 0, cut)
        reduce_1x(e)
        if then is not None:
            forward(then)
        into_gate_up(e, cut, tiles)
        reduce_1y(e)

    every = pl.ds(0, width)
    first(0)
    along_z(0)
    first(1)
    second(0)
    forward(0)
    w_copies[0].wait()
    w_copies[1].wait()
    ready(0)
    into_gate_up(0, 0, cut)
    reduce_1x(0)
    second(1)
    along_z(2)
    forward(1)
    into_gate_up(0, cut, tiles)
    reduce_1y(0)
    gate_up(1, 3)
    reduce_2(0)
    gate_up(3, 2)
    reduce_2(1)
    reduce_2b(0)
    gate_up(2)
    reduce_2(3)
    reduce_2b(1)
    reduce_3(0)
    reduce_2(2)
    reduce_2b(3)
    reduce_3(1)
    gather_2(0)
    reduce_2b(2)
    reduce_3(3)
    gather_2(1)
    gather_2b(0)
    reduce_3(2)
    gather_2(3)
    gather_2b(1)
    w_copies[2].wait()
    down(0)
    gather_2(2)
    gather_2b(3)
    down(1)
    out_2(0, 0, every)
    gather_2b(2)
    down(3)
    out_2(1, 1, every)
    out_3(1, 1, every)

    piece = width // PIECES
    blocks = [pl.ds(i * piece, piece) for i in range(PIECES)]
    down_ready(2)
    for i, cols in enumerate(blocks):
        down_tiles(2, i * piece // TILE, (i + 1) * piece // TILE)
        send(f"oc_2{i}", obuf.at[2, 1 - k, :, :, cols], rcore.at[2, :, :, cols], core_peer)
        if i == 0:
            out_2(3, 3, every)
    out_3(0, 0, every)
    for i, cols in enumerate(blocks):
        out_2(2, f"2{i}", cols)
        if i == 0:
            out_3(3, 3, every)
    for i, cols in enumerate(blocks):
        out_3(2, f"2{i}", cols)

    @pl.when(diagonal)
    def _():
        out_ref[...] = fin[...]

    for _, back in backs:

        @pl.when(jnp.logical_not(diagonal))
        def _():
            back.wait()

    for cp in sent:
        cp.wait_send()

    @pl.when(jnp.logical_not(diagonal))
    def _():
        turns[1].wait_send()

    for j in range(8):

        @pl.when(jnp.logical_not(jnp.logical_and(diagonal, j == r)))
        def _():
            sq_out[j].wait_send()


def feed_forward(index, residual, gain, gate_weight, up_weight, down_weight):
    rows, width = residual.shape
    hid = gate_weight.shape[1]
    both = 2 * hid
    split_in = both // TILE * 7 // 13 * TILE
    split_hid = hid // 128 * 6 // 13 * 128
    n_copies = 160
    cfg = dict(
        rows=rows,
        width=width,
        hid=hid,
        split_in=split_in,
        split_hid=split_hid,
        model=gain.shape[1],
        sq0=n_copies,
    )
    bf16 = jnp.bfloat16
    rest = both - split_in
    vmem = pl.BlockSpec(memory_space=pltpu.VMEM)
    hbm = pl.BlockSpec(memory_space=pl.ANY)
    scratch = [
        pltpu.VMEM((width, both), bf16),
        pltpu.VMEM((hid, width), bf16),
        pltpu.VMEM((1, width), jnp.float32),
        pltpu.VMEM((1, width), jnp.float32),
        pltpu.VMEM((8, 128), jnp.float32),
        pltpu.VMEM((rows, width), bf16),
        pltpu.VMEM((8, 8, 128), jnp.float32),
        pltpu.VMEM((4, 2, NZ, STRIPE, width), bf16),
        pltpu.VMEM((NZ, 2, NX, STRIPE, both), bf16),
        pltpu.VMEM((NZ, NX - 1, 2, STRIPE, split_in), bf16),
        pltpu.VMEM((NZ, 2, STRIPE, split_in), bf16),
        pltpu.VMEM((NZ, STRIPE, split_in), bf16),
        pltpu.VMEM((NZ, NX, STRIPE, rest), bf16),
        pltpu.VMEM((NZ, NX, STRIPE, rest), bf16),
        pltpu.VMEM((NZ, NX - 1, STRIPE, rest), bf16),
        pltpu.VMEM((NZ, 2, STRIPE, split_in), bf16),
        pltpu.VMEM((NZ, STRIPE, rest), bf16),
        pltpu.VMEM((NZ, 2, NX, STRIPE, hid), bf16),
        pltpu.VMEM((4, 2, NZ, STRIPE, width), bf16),
        pltpu.VMEM((4, NZ, STRIPE, width), bf16),
        pltpu.VMEM((4, NZ, STRIPE, width), bf16),
        pltpu.VMEM((4, NZ - 1, STRIPE, width), bf16),
        pltpu.VMEM((rows, width), bf16),
        pltpu.VMEM((rows, width), bf16),
        pltpu.VMEM((rows, width), bf16),
        pltpu.SemaphoreType.DMA((4,)),
        pltpu.SemaphoreType.DMA((n_copies + 8,)),
        pltpu.SemaphoreType.DMA((n_copies + 8,)),
        pltpu.SemaphoreType.DMA((2,)),
    ]
    return pl.pallas_call(
        functools.partial(ffn_kernel, cfg),
        out_shape=jax.ShapeDtypeStruct((rows, width), bf16),
        in_specs=[pl.BlockSpec(memory_space=pltpu.SMEM), vmem, hbm, hbm, hbm, hbm],
        out_specs=vmem,
        scratch_shapes=scratch,
        compiler_params=pltpu.CompilerParams(
            collective_id=0, has_side_effects=True, vmem_limit_bytes=60 * 2**20
        ),
    )(index, residual, gain, gate_weight, up_weight, down_weight)


def on_device(
    query_rows,
    key_cache,
    value_cache,
    cache_lengths,
    residual_in,
    norm_gain,
    outlier_index,
    gate_weight,
    up_weight,
    down_weight,
):
    rows_dev, width_dev = query_rows.shape
    cache_len = key_cache.shape[1]
    kv_local = key_cache.shape[2] // HD
    group_size = width_dev // HD // kv_local
    query_part = query_rows.reshape(rows_dev, kv_local, group_size, HD)
    key_part = key_cache.reshape(rows_dev, cache_len, kv_local, HD)
    value_part = value_cache.reshape(rows_dev, cache_len, kv_local, HD)
    scores = jnp.einsum(
        "igqd,itgd->igqt", query_part, key_part, preferred_element_type=jnp.float32
    ) * HD ** (-0.5)
    valid_mask = jnp.arange(cache_len, dtype=jnp.int32)[None, :] < cache_lengths[:, None]
    scores = jnp.where(valid_mask[:, None, None, :], scores, -1e30)
    top_score = jnp.max(scores, axis=-1, keepdims=True)
    expon = jnp.exp(scores - top_score)
    attn_probs = (expon / jnp.sum(expon, axis=-1, keepdims=True)).astype(jnp.bfloat16)
    attention = jnp.einsum(
        "igqt,itgd->igqd", attn_probs, value_part, preferred_element_type=jnp.float32
    ).reshape(rows_dev, width_dev)
    residual = (residual_in.astype(jnp.float32) + attention).astype(jnp.bfloat16)
    ffn = feed_forward(
        outlier_index, residual, norm_gain[None, :], gate_weight, up_weight, down_weight
    )
    return (residual.astype(jnp.float32) + ffn.astype(jnp.float32)).astype(jnp.bfloat16)


def solution(mesh):
    in_specs = (
        P(("side", "row"), "col"),
        P(("side", "row"), None, "col"),
        P(("side", "row"), None, "col"),
        P(("side", "row")),
        P(("side", "row"), "col"),
        P(),
        P(),
        P("row", ("side", "col")),
        P("row", ("side", "col")),
        P(("side", "col"), "row"),
    )
    out_specs = P(("side", "row"), "col")
    return jax.shard_map(
        on_device, mesh=mesh, in_specs=in_specs, out_specs=out_specs, check_vma=False
    )
```

time: 119 us -> 98 us (0.82)
  the two profiles are of different devices: /device:TPU:3 before, /device:TPU:7 now
where the time goes in v2:
time: 98 us; the launch traced here: 97.8 us
  Pallas kernels  90.1 us (92%)
  other arithmetic  3.47 us (4%)
  matrix products  3.19 us (3%)
    pallas_call x1, Pallas kernels, feed_forward(): pl.pallas_call(functools.partial(ffn_kernel, cfg), out_shape=jax.ShapeDty...  90.1 us
    dot_general x1, matrix products, on_device(): jnp.einsum('igqt,itgd->igqd', attn_probs, value_part, preferred_element_t...  2.54 us

profile of v2, /device:TPU:7, one launch (start us, length us, event | category | flops | bytes accessed | tf_op | source)
XLA Modules:
  0.0 97.8 jit_solution(12305295816240493736)
XLA Ops:
  0.0 0.0 copy-start
  0.0 0.9 iota_compare_fusion
  0.9 0.9 copy.11
  1.8 0.0 copy-done
  1.8 0.7 fusion.3
  2.5 0.0 copy-start.2
  2.5 0.2 fusion.8
  2.7 2.5 %fusion.4 = f32[32,16,128]{2,1,0:T(8,128)S(1)} fusion(bf16[32,256,128]{2,1,0:T(8,128)(2,1)} %param.12, f32[32,16]{1,0:T(8,128)S(1)} %fusion.8, f32[32,16,256]{2,1,0:T(8,128)S(1)} %fusion.3), kind=kOutput, calls=%fused_computation.6 | convolution fusion | flops 33948416 | bytes 2885632 | tf_op jit(solution)/shard_map/igqt,itgd->igqd/dot_general | solution.py:654
  5.3 0.0 copy-done.2
  5.3 0.8 fusion.5.res_ref
  6.0 0.0 copy-start.1
  6.0 90.1 %shard_map.100 = bf16[32,2048]{1,0:T(8,128)(2,1)} custom-call(s32[64]{0:T(128)} %index_ref.1, bf16[32,2048]{1,0:T(8,128)(2,1)} %fusion.5.res_ref, f32[1,16384]{1,0:T(1,128)} %bitcast.16, bf16[2048,1664]{1,0:T(8,128)(2,1)} %gate_hbm.1, bf16[2048,1664]{1,0:T(8,128)(2,1)} %up_hbm.1, bf16[1664,2048]{1,0:T(8,128)(2,1)} %down_hbm.1), custom_call_target="tpu_custom_call" | custom-call | tf_op jit(solution)/shard_map/pallas_call | solution.py:615
  96.2 0.0 copy-done.1
  96.2 1.6 %add_convert_fusion = bf16[32,2048]{1,0:T(8,128)(2,1)} fusion(bf16[32,2048]{1,0:T(8,128)(2,1)} %shard_map.100, bf16[32,2048]{1,0:T(8,128)(2,1)S(1)} %copy-done.1), kind=kLoop, calls=%fused_computation.9 | loop fusion | flops 262144 | bytes 393216 | tf_op jit(solution)/shard_map/convert_element_type | solution.py:661
Async XLA Ops:
  0.0 1.8 %copy-start = (bf16[32,256,128]{2,1,0:T(8,128)(2,1)S(1)}, bf16[32,256,128]{2,1,0:T(8,128)(2,1)}, u32[]{:S(2)}) copy-start(bf16[32,256,128]{2,1,0:T(8,128)(2,1)} %param.11) | copy-start | bytes 6291460
  2.5 2.8 %copy-start.2 = (bf16[32,2048]{1,0:T(8,128)(2,1)S(1)}, bf16[32,2048]{1,0:T(8,128)(2,1)}, u32[]{:S(2)}) copy-start(bf16[32,2048]{1,0:T(8,128)(2,1)} %param.14) | copy-start | bytes 393220
  6.0 90.2 %copy-start.1 = (bf16[32,2048]{1,0:T(8,128)(2,1)S(1)}, bf16[32,2048]{1,0:T(8,128)(2,1)}, u32[]{:S(2)}) copy-start(bf16[32,2048]{1,0:T(8,128)(2,1)} %fusion.5.res_ref) | copy-start | bytes 393220

commit v3 on v2

--- a/solution.py
+++ b/solution.py
@@ -469,10 +469,10 @@
         ready(e)
         into_gate_up(e, 0, cut)
         reduce_1x(e)
+        into_gate_up(e, cut, tiles)
+        reduce_1y(e)
         if then is not None:
             forward(then)
-        into_gate_up(e, cut, tiles)
-        reduce_1y(e)
 
     every = pl.ds(0, width)
     first(0)
@@ -485,16 +485,18 @@
     ready(0)
     into_gate_up(0, 0, cut)
     reduce_1x(0)
-    second(1)
-    along_z(2)
-    forward(1)
     into_gate_up(0, cut, tiles)
     reduce_1y(0)
-    gate_up(1, 3)
+    second(1)
+    forward(1)
+    along_z(2)
+    gate_up(1)
     reduce_2(0)
-    gate_up(3, 2)
+    forward(3)
+    gate_up(3)
     reduce_2(1)
     reduce_2b(0)
+    forward(2)
     gate_up(2)
     reduce_2(3)
     reduce_2b(1)
@@ -510,16 +512,15 @@
     reduce_3(2)
     gather_2(3)
     gather_2b(1)
+    gather_2(2)
+    gather_2b(3)
     w_copies[2].wait()
     down(0)
-    gather_2(2)
-    gather_2b(3)
     down(1)
+    gather_2b(2)
     out_2(0, 0, every)
-    gather_2b(2)
     down(3)
     out_2(1, 1, every)
-    out_3(1, 1, every)
 
     piece = width // PIECES
     blocks = [pl.ds(i * piece, piece) for i in range(PIECES)]
@@ -529,11 +530,12 @@
         send(f"oc_2{i}", obuf.at[2, 1 - k, :, :, cols], rcore.at[2, :, :, cols], core_peer)
         if i == 0:
             out_2(3, 3, every)
-    out_3(0, 0, every)
     for i, cols in enumerate(blocks):
         out_2(2, f"2{i}", cols)
         if i == 0:
-            out_3(3, 3, every)
+            out_3(1, 1, every)
+    out_3(3, 3, every)
+    out_3(0, 0, every)
     for i, cols in enumerate(blocks):
         out_3(2, f"2{i}", cols)
 

time: 98 us -> 95.2 us (0.971)
  Pallas kernels: 90.1 us -> 86.5 us
    pallas_call x1, Pallas kernels: 90.1 us -> 86.5 us  [feed_forward(): pl.pallas_call(functools.partial(ffn_kernel, cfg), out_shape=jax.ShapeDty...]
where the time goes in v3:
time: 95.2 us; the launch traced here: 94.1 us
  Pallas kernels  86.5 us (91%)
  other arithmetic  3.47 us (4%)
  matrix products  3.19 us (3%)
    pallas_call x1, Pallas kernels, feed_forward(): pl.pallas_call(functools.partial(ffn_kernel, cfg), out_shape=jax.ShapeDty...  86.5 us
    dot_general x1, matrix products, on_device(): jnp.einsum('igqt,itgd->igqd', attn_probs, value_part, preferred_element_t...  2.54 us

profile of v3, /device:TPU:7, one launch (start us, length us, event | category | flops | bytes accessed | tf_op | source)
XLA Modules:
  0.0 94.1 jit_solution(14434849445718893086)
XLA Ops:
  0.0 0.0 copy-start
  0.0 0.9 iota_compare_fusion
  0.9 0.9 copy.11
  1.8 0.0 copy-done
  1.8 0.7 fusion.3
  2.5 0.0 copy-start.2
  2.5 0.2 fusion.8
  2.7 2.5 %fusion.4 = f32[32,16,128]{2,1,0:T(8,128)S(1)} fusion(bf16[32,256,128]{2,1,0:T(8,128)(2,1)} %param.12, f32[32,16]{1,0:T(8,128)S(1)} %fusion.8, f32[32,16,256]{2,1,0:T(8,128)S(1)} %fusion.3), kind=kOutput, calls=%fused_computation.6 | convolution fusion | flops 33948416 | bytes 2885632 | tf_op jit(solution)/shard_map/igqt,itgd->igqd/dot_general | solution.py:656
  5.3 0.0 copy-done.2
  5.3 0.8 fusion.5.res_ref
  6.0 0.0 copy-start.1
  6.0 86.5 %shard_map.100 = bf16[32,2048]{1,0:T(8,128)(2,1)} custom-call(s32[64]{0:T(128)} %index_ref.1, bf16[32,2048]{1,0:T(8,128)(2,1)} %fusion.5.res_ref, f32[1,16384]{1,0:T(1,128)} %bitcast.16, bf16[2048,1664]{1,0:T(8,128)(2,1)} %gate_hbm.1, bf16[2048,1664]{1,0:T(8,128)(2,1)} %up_hbm.1, bf16[1664,2048]{1,0:T(8,128)(2,1)} %down_hbm.1), custom_call_target="tpu_custom_call" | custom-call | tf_op jit(solution)/shard_map/pallas_call | solution.py:617
  92.5 0.0 copy-done.1
  92.6 1.6 %add_convert_fusion = bf16[32,2048]{1,0:T(8,128)(2,1)} fusion(bf16[32,2048]{1,0:T(8,128)(2,1)} %shard_map.100, bf16[32,2048]{1,0:T(8,128)(2,1)S(1)} %copy-done.1), kind=kLoop, calls=%fused_computation.9 | loop fusion | flops 262144 | bytes 393216 | tf_op jit(solution)/shard_map/convert_element_type | solution.py:663
Async XLA Ops:
  0.0 1.8 %copy-start = (bf16[32,256,128]{2,1,0:T(8,128)(2,1)S(1)}, bf16[32,256,128]{2,1,0:T(8,128)(2,1)}, u32[]{:S(2)}) copy-start(bf16[32,256,128]{2,1,0:T(8,128)(2,1)} %param.11) | copy-start | bytes 6291460
  2.5 2.8 %copy-start.2 = (bf16[32,2048]{1,0:T(8,128)(2,1)S(1)}, bf16[32,2048]{1,0:T(8,128)(2,1)}, u32[]{:S(2)}) copy-start(bf16[32,2048]{1,0:T(8,128)(2,1)} %param.14) | copy-start | bytes 393220
  6.0 86.5 %copy-start.1 = (bf16[32,2048]{1,0:T(8,128)(2,1)S(1)}, bf16[32,2048]{1,0:T(8,128)(2,1)}, u32[]{:S(2)}) copy-start(bf16[32,2048]{1,0:T(8,128)(2,1)} %fusion.5.res_ref) | copy-start | bytes 393220

commit v4 on v3

--- a/solution.py
+++ b/solution.py
@@ -213,7 +213,7 @@
         send(f"g_s{h}", xbuf.at[2 * h, k, z], xbuf.at[2 * h + 1, k, z], side_peer)
 
     def along_z(e):
-        for d in (2, 1, 3):
+        for d in (1, 3, 2):
             send(f"g_z{e}_{d}", xbuf.at[e, k, z], xbuf.at[e, k, z], z_peer(d))
 
     def second(h):

time: 95.2 us -> 95.9 us (level)
  no operation moved by 1% of the time
where the time goes in v4:
time: 95.9 us; the launch traced here: 94.4 us
  Pallas kernels  86.7 us (90%)
  other arithmetic  3.47 us (4%)
  matrix products  3.19 us (3%)
    pallas_call x1, Pallas kernels, feed_forward(): pl.pallas_call(functools.partial(ffn_kernel, cfg), out_shape=jax.ShapeDty...  86.7 us
    dot_general x1, matrix products, on_device(): jnp.einsum('igqt,itgd->igqd', attn_probs, value_part, preferred_element_t...  2.54 us

profile of v4, /device:TPU:7, one launch (start us, length us, event | category | flops | bytes accessed | tf_op | source)
XLA Modules:
  0.0 94.4 jit_solution(6585801425202322812)
XLA Ops:
  0.0 0.0 copy-start
  0.0 0.9 iota_compare_fusion
  0.9 0.9 copy.11
  1.8 0.0 copy-done
  1.8 0.7 fusion.3
  2.5 0.0 copy-start.2
  2.5 0.2 fusion.8
  2.7 2.5 %fusion.4 = f32[32,16,128]{2,1,0:T(8,128)S(1)} fusion(bf16[32,256,128]{2,1,0:T(8,128)(2,1)} %param.12, f32[32,16]{1,0:T(8,128)S(1)} %fusion.8, f32[32,16,256]{2,1,0:T(8,128)S(1)} %fusion.3), kind=kOutput, calls=%fused_computation.6 | convolution fusion | flops 33948416 | bytes 2885632 | tf_op jit(solution)/shard_map/igqt,itgd->igqd/dot_general | solution.py:656
  5.3 0.0 copy-done.2
  5.3 0.8 fusion.5.res_ref
  6.0 0.0 copy-start.1
  6.0 86.7 %shard_map.100 = bf16[32,2048]{1,0:T(8,128)(2,1)} custom-call(s32[64]{0:T(128)} %index_ref.1, bf16[32,2048]{1,0:T(8,128)(2,1)} %fusion.5.res_ref, f32[1,16384]{1,0:T(1,128)} %bitcast.16, bf16[2048,1664]{1,0:T(8,128)(2,1)} %gate_hbm.1, bf16[2048,1664]{1,0:T(8,128)(2,1)} %up_hbm.1, bf16[1664,2048]{1,0:T(8,128)(2,1)} %down_hbm.1), custom_call_target="tpu_custom_call" | custom-call | tf_op jit(solution)/shard_map/pallas_call | solution.py:617
  92.8 0.0 copy-done.1
  92.8 1.6 %add_convert_fusion = bf16[32,2048]{1,0:T(8,128)(2,1)} fusion(bf16[32,2048]{1,0:T(8,128)(2,1)} %shard_map.100, bf16[32,2048]{1,0:T(8,128)(2,1)S(1)} %copy-done.1), kind=kLoop, calls=%fused_computation.9 | loop fusion | flops 262144 | bytes 393216 | tf_op jit(solution)/shard_map/convert_element_type | solution.py:663
Async XLA Ops:
  0.0 1.8 %copy-start = (bf16[32,256,128]{2,1,0:T(8,128)(2,1)S(1)}, bf16[32,256,128]{2,1,0:T(8,128)(2,1)}, u32[]{:S(2)}) copy-start(bf16[32,256,128]{2,1,0:T(8,128)(2,1)} %param.11) | copy-start | bytes 6291460
  2.5 2.8 %copy-start.2 = (bf16[32,2048]{1,0:T(8,128)(2,1)S(1)}, bf16[32,2048]{1,0:T(8,128)(2,1)}, u32[]{:S(2)}) copy-start(bf16[32,2048]{1,0:T(8,128)(2,1)} %param.14) | copy-start | bytes 393220
  6.0 86.8 %copy-start.1 = (bf16[32,2048]{1,0:T(8,128)(2,1)S(1)}, bf16[32,2048]{1,0:T(8,128)(2,1)}, u32[]{:S(2)}) copy-start(bf16[32,2048]{1,0:T(8,128)(2,1)} %fusion.5.res_ref) | copy-start | bytes 393220

commit v5 on v3

--- a/solution.py
+++ b/solution.py
@@ -567,8 +567,8 @@
     rows, width = residual.shape
     hid = gate_weight.shape[1]
     both = 2 * hid
-    split_in = both // TILE * 7 // 13 * TILE
-    split_hid = hid // 128 * 6 // 13 * 128
+    split_in = both // TILE * 8 // 13 * TILE
+    split_hid = hid // 128 * 5 // 13 * 128
     n_copies = 160
     cfg = dict(
         rows=rows,

time: 95.2 us -> 95.3 us (level)
  no operation moved by 1% of the time
where the time goes in v5:
time: 95.3 us; the launch traced here: 94.1 us
  Pallas kernels  86.5 us (91%)
  other arithmetic  3.47 us (4%)
  matrix products  3.19 us (3%)
    pallas_call x1, Pallas kernels, feed_forward(): pl.pallas_call(functools.partial(ffn_kernel, cfg), out_shape=jax.ShapeDty...  86.5 us
    dot_general x1, matrix products, on_device(): jnp.einsum('igqt,itgd->igqd', attn_probs, value_part, preferred_element_t...  2.54 us

profile of v5, /device:TPU:7, one launch (start us, length us, event | category | flops | bytes accessed | tf_op | source)
XLA Modules:
  0.0 94.1 jit_solution(14180192963133339989)
XLA Ops:
  0.0 0.0 copy-start
  0.0 0.9 iota_compare_fusion
  0.9 0.9 copy.11
  1.8 0.0 copy-done
  1.8 0.7 fusion.3
  2.5 0.0 copy-start.2
  2.5 0.2 fusion.8
  2.7 2.5 %fusion.4 = f32[32,16,128]{2,1,0:T(8,128)S(1)} fusion(bf16[32,256,128]{2,1,0:T(8,128)(2,1)} %param.12, f32[32,16]{1,0:T(8,128)S(1)} %fusion.8, f32[32,16,256]{2,1,0:T(8,128)S(1)} %fusion.3), kind=kOutput, calls=%fused_computation.6 | convolution fusion | flops 33948416 | bytes 2885632 | tf_op jit(solution)/shard_map/igqt,itgd->igqd/dot_general | solution.py:656
  5.3 0.0 copy-done.2
  5.3 0.8 fusion.5.res_ref
  6.0 0.0 copy-start.1
  6.0 86.5 %shard_map.100 = bf16[32,2048]{1,0:T(8,128)(2,1)} custom-call(s32[64]{0:T(128)} %index_ref.1, bf16[32,2048]{1,0:T(8,128)(2,1)} %fusion.5.res_ref, f32[1,16384]{1,0:T(1,128)} %bitcast.16, bf16[2048,1664]{1,0:T(8,128)(2,1)} %gate_hbm.1, bf16[2048,1664]{1,0:T(8,128)(2,1)} %up_hbm.1, bf16[1664,2048]{1,0:T(8,128)(2,1)} %down_hbm.1), custom_call_target="tpu_custom_call" | custom-call | tf_op jit(solution)/shard_map/pallas_call | solution.py:617
  92.5 0.0 copy-done.1
  92.5 1.6 %add_convert_fusion = bf16[32,2048]{1,0:T(8,128)(2,1)} fusion(bf16[32,2048]{1,0:T(8,128)(2,1)} %shard_map.100, bf16[32,2048]{1,0:T(8,128)(2,1)S(1)} %copy-done.1), kind=kLoop, calls=%fused_computation.9 | loop fusion | flops 262144 | bytes 393216 | tf_op jit(solution)/shard_map/convert_element_type | solution.py:663
Async XLA Ops:
  0.0 1.8 %copy-start = (bf16[32,256,128]{2,1,0:T(8,128)(2,1)S(1)}, bf16[32,256,128]{2,1,0:T(8,128)(2,1)}, u32[]{:S(2)}) copy-start(bf16[32,256,128]{2,1,0:T(8,128)(2,1)} %param.11) | copy-start | bytes 6291460
  2.5 2.8 %copy-start.2 = (bf16[32,2048]{1,0:T(8,128)(2,1)S(1)}, bf16[32,2048]{1,0:T(8,128)(2,1)}, u32[]{:S(2)}) copy-start(bf16[32,2048]{1,0:T(8,128)(2,1)} %param.14) | copy-start | bytes 393220
  6.0 86.5 %copy-start.1 = (bf16[32,2048]{1,0:T(8,128)(2,1)S(1)}, bf16[32,2048]{1,0:T(8,128)(2,1)}, u32[]{:S(2)}) copy-start(bf16[32,2048]{1,0:T(8,128)(2,1)} %fusion.5.res_ref) | copy-start | bytes 393220
